TPU v7x, 256 devices: a whole 4x4x8 slice. The times are simulated.
256 devices in a mesh: dp: 256 (over y, z, x, core).
Axes of the slice: x: 4, y: 4, z: 8, core: 2. Of those that a mesh axis runs over, the one named last changes fastest.
Arguments:
- image_feat: bfloat16 [131072, 1152], P('dp'), may hold values from -6 to 6
- text_feat: bfloat16 [131072, 1152], P('dp'), may hold values from -6 to 6
- image_proj: bfloat16 [1152, 1152], replicated, may hold values from -0.1875 to 0.1875
- text_proj: bfloat16 [1152, 1152], replicated, may hold values from -0.1875 to 0.1875
- logit_scale_logarithm: float32 [1], replicated, may hold values from 0 to 1.5
- bias: float32 [1], replicated, may hold values from -2 to 0
- counts: int32 [256], P('dp'), may hold values from 1 to 4, 512 in all
Outputs:
- image_proj_grad: float32 [1327104], P('dp')
- text_proj_grad: float32 [1327104], P('dp')
Inputs may be any that keep to these rules, and one draw needn't show every extreme that they name: counts holds whole pair blocks of 128 pairs; the counts sum to 512, and at least one device holds 4 blocks.
All inputs are finite; a program needn't handle non-finite values.
Results may differ from a plain program's by a relative error of at most 0.0043.
Values may be sent and summed in bfloat16 or wider, within the bound.
No kernel may reach another device: no remote copies, remote signals or barrier semaphores. Data moves between devices by JAX's collectives and lax.ppermute only.
A program may use at most 128 MiB of HBM per device.

v0:
```python
import jax
import jax.numpy as jnp
from jax import lax
from jax.sharding import PartitionSpec as P

BLK = 128
STEPS = 4


def from_behind(value, axis, steps):
    count = lax.axis_size(axis)
    pairs = [(source, (source + steps) % count) for source in range(count)]
    return lax.ppermute(value, axis, pairs)


def project_rows(features, weight_tensors):
    projected = jnp.dot(features, weight_tensors, preferred_element_type=jnp.float32)
    row_norm = jnp.sqrt(jnp.sum(projected * projected, axis=1, keepdims=True) + 1e-06)
    return (projected / row_norm, row_norm)


def raw_grad(gradient, direction, row_norm):
    radial = jnp.sum(direction * gradient, axis=1, keepdims=True)
    return ((gradient - direction * radial) / row_norm).astype(jnp.bfloat16)


def weight_term(features, delta):
    return lax.dot_general(
        features, delta, (((0,), (0,)), ((), ())), preferred_element_type=jnp.float32
    )


def live_rows(count_tag, total_rows):
    slot_index = lax.iota(jnp.int32, total_rows)
    return slot_index.astype(jnp.float32) < count_tag[0].astype(jnp.float32) * BLK


def pass_texts(caption_block_rows, text_count):
    return from_behind((caption_block_rows, text_count), "dp", 1)


def pairing_weight_matrix(
    picture_unit_vector,
    picture_valid_rows,
    caption_block_rows,
    caption_valid_rows,
    softness_factor,
    shard_displacement,
    including_matches,
):
    cosine_affinity = lax.dot_general(
        picture_unit_vector,
        caption_block_rows,
        (((1,), (1,)), ((), ())),
        preferred_element_type=jnp.float32,
    )
    pair_logit_matrix = softness_factor * cosine_affinity + shard_displacement
    if including_matches:
        row_index = lax.iota(jnp.int32, picture_unit_vector.shape[0])
        col_index = lax.iota(jnp.int32, caption_block_rows.shape[0])
        positive = row_index[:, None] == col_index[None, :]
        weight_tensors = jnp.where(
            positive, -jax.nn.sigmoid(-pair_logit_matrix), jax.nn.sigmoid(pair_logit_matrix)
        )
    else:
        weight_tensors = jax.nn.sigmoid(pair_logit_matrix)
    return jnp.where(
        picture_valid_rows[:, None] & caption_valid_rows[None, :], weight_tensors, 0.0
    ).astype(jnp.bfloat16)


def picture_portion(weight_tensors, caption_block_rows, softness_factor):
    return softness_factor * jnp.dot(
        weight_tensors, caption_block_rows, preferred_element_type=jnp.float32
    )


def caption_portion(weight_tensors, picture_block_rows, softness_factor):
    return softness_factor * lax.dot_general(
        weight_tensors,
        picture_block_rows,
        (((0,), (0,)), ((), ())),
        preferred_element_type=jnp.float32,
    )


def local(image_feat, text_feat, image_proj, text_proj, logit_scale_logarithm, bias, counts):
    softness_factor = jnp.exp(logit_scale_logarithm[0])
    shard_displacement = bias[0]
    image_dir, image_norm = project_rows(image_feat, image_proj)
    text_dir, text_norm = project_rows(text_feat, text_proj)
    picture_unit_vector = image_dir.astype(jnp.bfloat16)
    caption_unit_vector = text_dir.astype(jnp.bfloat16)
    total_rows = image_feat.shape[0]
    count_tag = counts.astype(jnp.bfloat16)
    local_valid_rows = live_rows(count_tag, total_rows)
    leading_entry = pairing_weight_matrix(
        picture_unit_vector,
        local_valid_rows,
        caption_unit_vector,
        local_valid_rows,
        softness_factor,
        shard_displacement,
        True,
    )
    picture_gradient = picture_portion(leading_entry, caption_unit_vector, softness_factor)
    incomplete_value = caption_portion(leading_entry, picture_unit_vector, softness_factor)
    caption_block_rows, text_count = (caption_unit_vector, count_tag)
    for cycle_step in range(1, STEPS):
        caption_block_rows, text_count = pass_texts(caption_block_rows, text_count)
        incomplete_value = from_behind(incomplete_value, "dp", 1)
        weight_tensors = pairing_weight_matrix(
            picture_unit_vector,
            local_valid_rows,
            caption_block_rows,
            live_rows(text_count, total_rows),
            softness_factor,
            shard_displacement,
            False,
        )
        picture_gradient = picture_gradient + picture_portion(
            weight_tensors, caption_block_rows, softness_factor
        )
        incomplete_value = incomplete_value + caption_portion(
            weight_tensors, picture_unit_vector, softness_factor
        )
    image_delta = raw_grad(picture_gradient, image_dir, image_norm)
    image_weight_grad = weight_term(image_feat, image_delta)
    returned = from_behind(incomplete_value, "dp", -(STEPS - 1))
    text_delta = raw_grad(returned, text_dir, text_norm)
    text_weight_grad = weight_term(text_feat, text_delta)
    image_out, text_out = (
        lax.psum_scatter(image_weight_grad.reshape(-1), "dp", scatter_dimension=0, tiled=True),
        lax.psum_scatter(text_weight_grad.reshape(-1), "dp", scatter_dimension=0, tiled=True),
    )
    return (image_out, text_out)


def solution(mesh):
    return jax.shard_map(
        local,
        mesh=mesh,
        in_specs=(P("dp", None), P("dp", None), P(), P(), P(), P(), P("dp")),
        out_specs=(P("dp"), P("dp")),
        check_vma=False,
    )
```

profile of v0, /device:TPU:1, one launch (start us, length us, event | category | flops | bytes accessed | tf_op | source)
XLA Modules:
  0.0 540.7 jit_solution(14752388516736088856)
XLA Ops:
  8.0 3.4 collective-permute-start
  11.5 3.2 multiply_reduce_fusion.3
  14.7 2.0 multiply_reduce_fusion.2
  19.1 2.8 collective-permute-done.2
  22.2 8.2 %collective-permute-done.4 = bf16[1]{0:T(256)(128)(2,1)} collective-permute-done((bf16[1]{0:T(256)(128)(2,1)}, bf16[1]{0:T(256)(128)(2,1)}, u32[]{:S(2)}, u32[]{:S(2)}) %collective-permute-start.4) | collective-permute-done | bytes 34 | tf_op jit(solution)/shard_map/ppermute | solution.py:13
  34.0 37.7 %collective-permute-done.1 = bf16[512,1152]{1,0:T(8,128)(2,1)S(1)} collective-permute-done((bf16[512,1152]{1,0:T(8,128)(2,1)S(1)}, bf16[512,1152]{1,0:T(8,128)(2,1)S(1)}, u32[]{:S(2)}, u32[]{:S(2)}) %collective-permute-start.1) | collective-permute-done | bytes 1179680 | tf_op jit(solution)/shard_map/ppermute | solution.py:13
  73.6 2.6 collective-permute-start.7
  77.0 37.6 %collective-permute-done.3 = bf16[512,1152]{1,0:T(8,128)(2,1)S(1)} collective-permute-done((bf16[512,1152]{1,0:T(8,128)(2,1)S(1)}, bf16[512,1152]{1,0:T(8,128)(2,1)S(1)}, u32[]{:S(2)}, u32[]{:S(2)}) %collective-permute-start.3) | collective-permute-done | bytes 1179680 | tf_op jit(solution)/shard_map/ppermute | solution.py:13
  116.8 2.6 collective-permute-start.8
  119.5 38.3 %collective-permute-done.5 = bf16[512,1152]{1,0:T(8,128)(2,1)S(1)} collective-permute-done((bf16[512,1152]{1,0:T(8,128)(2,1)S(1)}, bf16[512,1152]{1,0:T(8,128)(2,1)S(1)}, u32[]{:S(2)}, u32[]{:S(2)}) %collective-permute-start.5) | collective-permute-done | bytes 1179680 | tf_op jit(solution)/shard_map/ppermute | solution.py:13
  159.8 1.6 add.88
  161.4 6.4 %collective-permute-start.9 = (f32[512,1152]{1,0:T(8,128)}, f32[512,1152]{1,0:T(8,128)}, u32[]{:S(2)}, u32[]{:S(2)}) collective-permute-start(f32[512,1152]{1,0:T(8,128)} %add.88), channel_id=1, source_target_pairs={{0,253},{1,254},{2,255},{3,0},{4,1},{5,2},{6,3},{7,4},{8,5},{9,6},... | collective-permute-start | bytes 7077896 | tf_op jit(solution)/shard_map/ppermute | solution.py:13
  170.4 1.2 multiply_reduce_fusion.1
  171.6 4.4 convolution_bitcast_fusion.1
  176.0 6.9 %copy.11 = f32[1152,1152]{1,0:T(8,128)} copy(f32[1152,1152]{0,1:T(8,128)} %convolution_bitcast_fusion.1) | data formatting | bytes 10616832 | tf_op jit(solution)/shard_map/dot_general | solution.py:28
  182.9 6.7 %reshape.56 = f32[1327104]{0:T(1024)} reshape(f32[1152,1152]{1,0:T(8,128)} %copy.11) | data formatting | bytes 10616832 | tf_op jit(solution)/shard_map/reshape | solution.py:133
  189.6 11.8 %collective-permute-done.9 = f32[512,1152]{1,0:T(8,128)} collective-permute-done((f32[512,1152]{1,0:T(8,128)}, f32[512,1152]{1,0:T(8,128)}, u32[]{:S(2)}, u32[]{:S(2)}) %collective-permute-start.9) | collective-permute-done | bytes 2359328 | tf_op jit(solution)/shard_map/ppermute | solution.py:13
  201.4 2.0 multiply_reduce_fusion
  203.5 6.0 %convolution_bitcast_fusion = f32[1152,1152]{0,1:T(8,128)} fusion(bf16[512,1152]{1,0:T(8,128)(2,1)S(1)} %copy-done.7, f32[512,1152]{1,0:T(8,128)} %collective-permute-done.9, f32[512]{0:T(512)S(1)} %multiply_reduce_fusion, f32[512]{0:T(512)S(1)} %add_sqrt_fusion, f32[512,1152]{1,0:T(8,128)S(1)} %copy-done.3), kind=kOutput, calls=%fused_computation | convolution fusion | flops 1361903616 | bytes 11210752 | tf_op jit(solution)/shard_map/dot_general | solution.py:28
  209.5 6.9 %copy.12 = f32[1152,1152]{1,0:T(8,128)} copy(f32[1152,1152]{0,1:T(8,128)} %convolution_bitcast_fusion) | data formatting | bytes 10616832 | tf_op jit(solution)/shard_map/dot_general | solution.py:28
  216.4 6.6 %reshape.57 = f32[1327104]{0:T(1024)} reshape(f32[1152,1152]{1,0:T(8,128)} %copy.12) | data formatting | bytes 10616832 | tf_op jit(solution)/shard_map/reshape | solution.py:134
  223.0 307.9 %all-reduce.5.cloned.1.call-done = (f32[1327104]{0:T(1024)}, f32[1327104]{0:T(1024)}) async-done(((f32[1327104]{0:T(1024)}, f32[1327104]{0:T(1024)}), (f32[1327104]{0:T(1024)}, f32[1327104]{0:T(1024)})) %all-reduce.5.cloned.1.call-update) | async-done | bytes 10616848
  530.9 1.4 dynamic-slice
  532.4 1.4 dynamic-slice.1
  (47 shorter events, 12.7 us)
Async XLA Ops:
  7.2 4.3 copy-start
  7.2 523.8 %all-reduce.5.cloned.1.call-start = ((), (), s32[]{:S(2)}) async-start(), calls=%async_computation | async-start | bytes 21233664
  8.0 6.7 %copy-start.4 = (bf16[1152,1152]{1,0:T(8,128)(2,1)S(1)}, bf16[1152,1152]{1,0:T(8,128)(2,1)}, u32[]{:S(2)}) copy-start(bf16[1152,1152]{1,0:T(8,128)(2,1)} %param.10) | copy-start | bytes 7962628
  8.0 6.7 %copy-start.6 = (bf16[512,1152]{1,0:T(8,128)(2,1)S(1)}, bf16[512,1152]{1,0:T(8,128)(2,1)}, u32[]{:S(2)}) copy-start(bf16[512,1152]{1,0:T(8,128)(2,1)} %param.8) | copy-start | bytes 3538948
  8.0 10.6 %collective-permute-start = (bf16[1]{0:T(256)(128)(2,1)}, bf16[1]{0:T(256)(128)(2,1)}, u32[]{:S(2)}, u32[]{:S(2)}) collective-permute-start(bf16[1]{0:T(256)(128)(2,1)} %convert_element_type.73), channel_id=1, source_target_pairs={{0,1},{1,2},{2,3},{3,4},{4,5},{5,6},{6,7},{7,8},{8,9},{9,10},{10,1... | collective-permute-start | bytes 14 | tf_op jit(solution)/shard_map/ppermute | solution.py:13
  16.6 2.0 copy-start.2
  18.7 3.2 collective-permute-start.2
  21.9 8.6 %collective-permute-start.4 = (bf16[1]{0:T(256)(128)(2,1)}, bf16[1]{0:T(256)(128)(2,1)}, u32[]{:S(2)}, u32[]{:S(2)}) collective-permute-start(bf16[1]{0:T(256)(128)(2,1)} %collective-permute-done.2), channel_id=1, source_target_pairs={{0,1},{1,2},{2,3},{3,4},{4,5},{5,6},{6,7},{7,8},{8,9},{9,10},{10,1... | collective-permute-start | bytes 14 | tf_op jit(solution)/shard_map/ppermute | solution.py:13
  33.1 39.6 %collective-permute-start.6 = (f32[512,1152]{1,0:T(8,128)S(1)}, f32[512,1152]{1,0:T(8,128)S(1)}, u32[]{:S(2)}, u32[]{:S(2)}) collective-permute-start(f32[512,1152]{1,0:T(8,128)S(1)} %convolution_multiply_fusion.3), channel_id=1, source_target_pairs={{0,1},{1,2},{2,3},{3,4},{4,5},{5,6},{6,7},{7,8},{8,9},{9,10},{10,1... | collective-permute-start | bytes 7077896 | tf_op jit(solution)/shard_map/ppermute | solution.py:13
  33.2 38.4 %collective-permute-start.1 = (bf16[512,1152]{1,0:T(8,128)(2,1)S(1)}, bf16[512,1152]{1,0:T(8,128)(2,1)S(1)}, u32[]{:S(2)}, u32[]{:S(2)}) collective-permute-start(bf16[512,1152]{1,0:T(8,128)(2,1)S(1)} %fusion.29), channel_id=1, source_target_pairs={{0,1},{1,2},{2,3},{3,4},{4,5},{5,6},{6,7},{7,8},{8,9},{9,10},{10,1... | collective-permute-start | bytes 3538952 | tf_op jit(solution)/shard_map/ppermute | solution.py:13
  73.6 43.0 %collective-permute-start.7 = (f32[512,1152]{1,0:T(8,128)S(1)}, f32[512,1152]{1,0:T(8,128)S(1)}, u32[]{:S(2)}, u32[]{:S(2)}) collective-permute-start(f32[512,1152]{1,0:T(8,128)S(1)} %fusion.1), channel_id=1, source_target_pairs={{0,1},{1,2},{2,3},{3,4},{4,5},{5,6},{6,7},{7,8},{8,9},{9,10},{10,1... | collective-permute-start | bytes 7077896 | tf_op jit(solution)/shard_map/ppermute | solution.py:13
  76.2 38.4 %collective-permute-start.3 = (bf16[512,1152]{1,0:T(8,128)(2,1)S(1)}, bf16[512,1152]{1,0:T(8,128)(2,1)S(1)}, u32[]{:S(2)}, u32[]{:S(2)}) collective-permute-start(bf16[512,1152]{1,0:T(8,128)(2,1)S(1)} %collective-permute-done.1), channel_id=1, source_target_pairs={{0,1},{1,2},{2,3},{3,4},{4,5},{5,6},{6,7},{7,8},{8,9},{9,10},{10,1... | collective-permute-start | bytes 3538952 | tf_op jit(solution)/shard_map/ppermute | solution.py:13
  116.8 43.0 %collective-permute-start.8 = (f32[512,1152]{1,0:T(8,128)S(1)}, f32[512,1152]{1,0:T(8,128)S(1)}, u32[]{:S(2)}, u32[]{:S(2)}) collective-permute-start(f32[512,1152]{1,0:T(8,128)S(1)} %add.87), channel_id=1, source_target_pairs={{0,1},{1,2},{2,3},{3,4},{4,5},{5,6},{6,7},{7,8},{8,9},{9,10},{10,1... | collective-permute-start | bytes 7077896 | tf_op jit(solution)/shard_map/ppermute | solution.py:13
  119.4 38.4 %collective-permute-start.5 = (bf16[512,1152]{1,0:T(8,128)(2,1)S(1)}, bf16[512,1152]{1,0:T(8,128)(2,1)S(1)}, u32[]{:S(2)}, u32[]{:S(2)}) collective-permute-start(bf16[512,1152]{1,0:T(8,128)(2,1)S(1)} %collective-permute-done.3), channel_id=1, source_target_pairs={{0,1},{1,2},{2,3},{3,4},{4,5},{5,6},{6,7},{7,8},{8,9},{9,10},{10,1... | collective-permute-start | bytes 3538952 | tf_op jit(solution)/shard_map/ppermute | solution.py:13
  161.4 40.0 %collective-permute-start.9 = (f32[512,1152]{1,0:T(8,128)}, f32[512,1152]{1,0:T(8,128)}, u32[]{:S(2)}, u32[]{:S(2)}) collective-permute-start(f32[512,1152]{1,0:T(8,128)} %add.88), channel_id=1, source_target_pairs={{0,253},{1,254},{2,255},{3,0},{4,1},{5,2},{6,3},{7,4},{8,5},{9,6},... | collective-permute-start | bytes 7077896 | tf_op jit(solution)/shard_map/ppermute | solution.py:13
  170.4 1.3 copy-start.5
  182.9 18.5 %copy-start.3 = (f32[512,1152]{1,0:T(8,128)S(1)}, f32[512,1152]{1,0:T(8,128)}, u32[]{:S(2)}) copy-start(f32[512,1152]{1,0:T(8,128)} %copy-done.2) | copy-start | bytes 7077892
  189.6 13.8 %copy-start.7 = (bf16[512,1152]{1,0:T(8,128)(2,1)S(1)}, bf16[512,1152]{1,0:T(8,128)(2,1)}, u32[]{:S(2)}) copy-start(bf16[512,1152]{1,0:T(8,128)(2,1)} %param.8) | copy-start | bytes 3538948
  223.0 310.8 %copy-start.1 = (bf16[1152,1152]{1,0:T(8,128)(2,1)S(1)}, bf16[1152,1152]{1,0:T(8,128)(2,1)}, u32[]{:S(2)}) copy-start(bf16[1152,1152]{1,0:T(8,128)(2,1)} %param.9) | copy-start | bytes 7962628
Sparse Core Ops, SparseCore 0:
  223.1 307.7 all-reduce.4
where the time goes:
time: 542 us; the launch traced here: 541 us
  waiting for transfers between devices  444 us (82%)
  local copies, waits for them, and re-layouts  30 us (6%)
  matrix products  27.2 us (5%)
  between operations  18.4 us (3%)
  starting transfers between devices  16.2 us (3%)
    unnamed x2, waiting for transfers between devices  308 us
    ppermute x10, waiting for transfers between devices, from_behind(): return lax.ppermute(value, axis, pairs)  136 us
    ppermute x10, starting transfers between devices, from_behind(): return lax.ppermute(value, axis, pairs)  16.1 us
    dot_general x2, local copies, waits for them, and re-layouts, weight_term(): lax.dot_general(features, delta, (((0,), (0,)), ((), ())), preferred_elem...  13.8 us
  transfers between devices with their start and end apart: 11, of which 7 were waited for; matrix products, arithmetic and copies ran while one was open for 6% of the time, Pallas kernels for 0%

commit v1 on v0

v1 whole, which is shorter than its diff:
```python
import jax
import jax.numpy as jnp
from jax import lax
from jax.sharding import PartitionSpec as P

BLK = 128
D = 1152
NY, NZ, NX = 4, 8, 4
N = 256
BF = jnp.bfloat16
F32 = jnp.float32


def dev(y, z, x, c):
    return ((y * NZ + z) * NX + x) * 2 + c


PLANES = [
    [dev(y, z, x, c) for y in range(NY) for x in range(NX)]
    for z in range(NZ)
    for c in range(2)
]
COLUMNS = [
    [dev(y, z, x, c) for z in range(NZ)]
    for y in range(NY)
    for x in range(NX)
    for c in range(2)
]
SWAP = [(d, d ^ 1) for d in range(N)]


def shift(value, steps):
    return lax.ppermute(value, "dp", [(d, (d + steps) % N) for d in range(N)])


def mm(a, b):
    return jnp.dot(a, b, preferred_element_type=F32)


def mm_t(a, b):
    return lax.dot_general(a, b, (((1,), (1,)), ((), ())), preferred_element_type=F32)


def t_mm(a, b):
    return lax.dot_general(a, b, (((0,), (0,)), ((), ())), preferred_element_type=F32)


def project_rows(features, proj):
    projected = mm(features, proj)
    norm = jnp.sqrt(jnp.sum(projected * projected, axis=1, keepdims=True) + 1e-06)
    return projected / norm, norm


def raw_grad(gradient, direction, norm):
    radial = jnp.sum(direction * gradient, axis=1, keepdims=True)
    return ((gradient - direction * radial) / norm).astype(BF)


def pair_weight(image_unit, text_unit, scale, bias, matches):
    logit = scale * mm_t(image_unit, text_unit) + bias
    if matches:
        rows = lax.broadcasted_iota(jnp.int32, logit.shape, 0)
        cols = lax.broadcasted_iota(jnp.int32, logit.shape, 1)
        weight = jnp.where(rows == cols, -jax.nn.sigmoid(-logit), jax.nn.sigmoid(logit))
    else:
        weight = jax.nn.sigmoid(logit)
    return weight.astype(BF)


def local(image_feat, text_feat, image_proj, text_proj, logit_scale_logarithm, bias, counts):
    scale = jnp.exp(logit_scale_logarithm[0])
    offset = bias[0]
    rows = lax.broadcasted_iota(jnp.int32, image_feat.shape, 0)
    live = rows < counts[0] * BLK
    zero = jnp.zeros((), BF)
    text0 = jnp.where(live, text_feat, zero)
    image0 = jnp.where(live, image_feat, zero)
    text2 = shift(text0, 2)
    image1 = shift(image0, -1)

    dir_i0, n_i0 = project_rows(image0, image_proj)
    dir_t0, n_t0 = project_rows(text0, text_proj)
    u_i0, u_t0 = dir_i0.astype(BF), dir_t0.astype(BF)
    w = pair_weight(u_i0, u_t0, scale, offset, True)
    g_i0 = mm(w, u_t0)
    g_t0 = t_mm(w, u_i0)

    dir_i1, n_i1 = project_rows(image1, image_proj)
    u_i1 = dir_i1.astype(BF)
    w = pair_weight(u_i1, u_t0, scale, offset, False)
    g_i1 = mm(w, u_t0)
    g_t0 = g_t0 + t_mm(w, u_i1)
    d_t0 = raw_grad(scale * g_t0, dir_t0, n_t0)
    term_t = t_mm(text0, d_t0)

    dir_t2, n_t2 = project_rows(text2, text_proj)
    u_t2 = dir_t2.astype(BF)
    w0 = pair_weight(u_i0, u_t2, scale, offset, False)
    w1 = pair_weight(u_i1, u_t2, scale, offset, False)
    g_i0 = g_i0 + mm(w0, u_t2)
    g_i1 = g_i1 + mm(w1, u_t2)
    g_t2 = t_mm(w0, u_i0) + t_mm(w1, u_i1)
    term_t = term_t + t_mm(text2, raw_grad(scale * g_t2, dir_t2, n_t2))
    term_i = t_mm(image0, raw_grad(scale * g_i0, dir_i0, n_i0)) + t_mm(
        image1, raw_grad(scale * g_i1, dir_i1, n_i1)
    )

    core = lax.axis_index("dp") % 2
    first = core == 0
    away = jnp.where(first, term_t, term_i).astype(BF)
    kept = jnp.where(first, term_i, term_t)
    chip = (kept + lax.ppermute(away, "dp", SWAP).astype(F32)).astype(BF)
    chip = chip.reshape(NY, NZ, NX, 9, D).transpose(0, 2, 1, 3, 4).reshape(16, 72, D)
    plane = lax.all_to_all(chip, "dp", 0, 0, axis_index_groups=PLANES, tiled=True)
    plane = jnp.sum(plane.astype(F32), axis=0).astype(BF).reshape(NZ, 9, D)
    column = lax.all_to_all(plane, "dp", 0, 0, axis_index_groups=COLUMNS, tiled=True)
    total = jnp.sum(column.astype(F32), axis=0).reshape(2, 9 * D // 2)
    mine = lax.dynamic_index_in_dim(total, core, 0, False)
    other = lax.ppermute(lax.dynamic_index_in_dim(total, 1 - core, 0, False), "dp", SWAP)
    return jnp.where(first, mine, other), jnp.where(first, other, mine)


def solution(mesh):
    return jax.shard_map(
        local,
        mesh=mesh,
        in_specs=(P("dp", None), P("dp", None), P(), P(), P(), P(), P("dp")),
        out_specs=(P("dp"), P("dp")),
        check_vma=False,
    )
```

time: 542 us -> 152 us (0.28)
  waiting for transfers between devices: 444 us -> 25.1 us
  blocking collectives: 0 us -> 38.7 us
  between operations: 18.4 us -> 3 us
  local copies, waits for them, and re-layouts: 30 us -> 15.7 us
  matrix products: 27.2 us -> 41.1 us
    unnamed x2 -> x0, waiting for transfers between devices: 308 us -> none
    ppermute x10 -> x4, waiting for transfers between devices: 136 us -> 14.6 us  [the longest x2 9.16 us: shift(): return lax.ppermute(value, 'dp', [(d, (d + steps) % N) for d in range(N)])]
    all_to_all x0 -> x1, blocking collectives: none -> 38.7 us  [local(): lax.all_to_all(chip, 'dp', 0, 0, axis_index_groups=PLANES, tiled=True)]
    dot_general x16 -> x20, matrix products: 27.2 us -> 41.1 us  [the longest x8 19.5 us: mm(): return jnp.dot(a, b, preferred_element_type=F32)]
    dot_general x2 -> x0, local copies, waits for them, and re-layouts: 13.8 us -> none  [weight_term(): lax.dot_general(features, delta, (((0,), (0,)), ((), ())), preferred_elem...]
    all_to_all x0 -> x1, waiting for transfers between devices: none -> 10.5 us  [local(): lax.all_to_all(plane, 'dp', 0, 0, axis_index_groups=COLUMNS, tiled=True)]
    ppermute x10 -> x4, starting transfers between devices: 16.1 us -> 14.1 us  [the longest x1 7.84 us: local(): chip = (kept + lax.ppermute(away, 'dp', SWAP).astype(F32)).astype(BF)]
    reshape x2 -> x5, local copies, waits for them, and re-layouts: 13.3 us -> 14.8 us  [the longest x3 13.9 us: local(): chip.reshape(NY, NZ, NX, 9, D).transpose(0, 2, 1, 3, 4).reshape(16, 72, D)]
  transfers between devices with their start and end apart: 11 -> 5, of which waited for: 7 -> 5; matrix products, arithmetic and copies ran while one was open for 6% -> 12% of each run, Pallas kernels for 0% -> 0%
where the time goes in v1:
time: 152 us; the launch traced here: 151 us
  matrix products  41.1 us (27%)
  blocking collectives  38.7 us (25%)
  waiting for transfers between devices  25.1 us (17%)
  starting transfers between devices  17.5 us (12%)
  local copies, waits for them, and re-layouts  15.7 us (10%)
  other arithmetic  9.72 us (6%)
  between operations  3 us (2%)
    all_to_all x1, blocking collectives, local(): lax.all_to_all(chip, 'dp', 0, 0, axis_index_groups=PLANES, tiled=True)  38.7 us
    dot_general x8, matrix products, mm(): return jnp.dot(a, b, preferred_element_type=F32)  19.5 us
    dot_general x8, matrix products, t_mm(): lax.dot_general(a, b, (((0,), (0,)), ((), ())), preferred_element_type=F32)  17.3 us
    reshape x3, local copies, waits for them, and re-layouts, local(): chip.reshape(NY, NZ, NX, 9, D).transpose(0, 2, 1, 3, 4).reshape(16, 72, D)  13.9 us
    all_to_all x1, waiting for transfers between devices, local(): lax.all_to_all(plane, 'dp', 0, 0, axis_index_groups=COLUMNS, tiled=True)  10.5 us
    ppermute x2, waiting for transfers between devices, shift(): return lax.ppermute(value, 'dp', [(d, (d + steps) % N) for d in range(N)])  9.16 us
    ppermute x1, starting transfers between devices, local(): chip = (kept + lax.ppermute(away, 'dp', SWAP).astype(F32)).astype(BF)  7.84 us
    ppermute x1, waiting for transfers between devices, local(): chip = (kept + lax.ppermute(away, 'dp', SWAP).astype(F32)).astype(BF)  4.58 us
  transfers between devices with their start and end apart: 5, of which 5 were waited for; matrix products, arithmetic and copies ran while one was open for 12% of the time, Pallas kernels for 0%

profile of v1, /device:TPU:1, one launch (start us, length us, event | category | flops | bytes accessed | tf_op | source)
XLA Modules:
  0.0 150.9 jit_solution(5254161459636226443)
XLA Ops:
  1.5 3.4 %broadcast_select_fusion.1 = (bf16[512,1152]{1,0:T(8,128)(2,1)}, bf16[512,1152]{1,0:T(8,128)(2,1)}) fusion(bf16[512,1152]{1,0:T(8,128)(2,1)} %param.7, pred[512]{0:T(512)(128)(4,1)S(1)} %iota_compare_fusion.1, bf16[512,1152]{1,0:T(8,128)(2,1)} %param.8), kind=kLoop, calls=%fused_computation.62 | loop fusion | flops 1179648 | bytes 4719104 | tf_op jit(solution)/shard_map/jit(_where)/select_n | solution.py:77
  4.8 3.2 %collective-permute-start.1 = (bf16[512,1152]{1,0:T(8,128)(2,1)}, bf16[512,1152]{1,0:T(8,128)(2,1)}, u32[]{:S(2)}, u32[]{:S(2)}) collective-permute-start(bf16[512,1152]{1,0:T(8,128)(2,1)} %get-tuple-element.6), channel_id=1, source_target_pairs={{0,255},{1,0},{2,1},{3,2},{4,3},{5,4},{6,5},{7,6},{8,7},{9,8},{10,... | collective-permute-start | bytes 3538952 | tf_op jit(solution)/shard_map/ppermute | solution.py:33
  8.1 4.7 %multiply_reduce_fusion.7 = (f32[512]{0:T(512)S(1)}, f32[512,1152]{1,0:T(8,128)}) fusion(bf16[512,1152]{1,0:T(8,128)(2,1)} %get-tuple-element.6, bf16[1152,1152]{1,0:T(8,128)(2,1)S(1)} %copy-done), kind=kOutput, calls=%fused_computation.23 | convolution fusion | flops 1360133632 | bytes 6195200 | tf_op jit(solution)/shard_map/dot_general | solution.py:37
  12.8 4.5 %multiply_reduce_fusion.6 = (f32[512]{0:T(512)S(1)}, f32[512,1152]{1,0:T(8,128)}) fusion(bf16[512,1152]{1,0:T(8,128)(2,1)} %get-tuple-element.7, bf16[1152,1152]{1,0:T(8,128)(2,1)S(1)} %copy-done.4), kind=kOutput, calls=%fused_computation.22 | convolution fusion | flops 1360133632 | bytes 6195200 | tf_op jit(solution)/shard_map/dot_general | solution.py:37
  18.6 1.9 %fusion.33 = bf16[512,1152]{1,0:T(8,128)(2,1)S(1)} fusion(f32[512,1152]{1,0:T(8,128)} %get-tuple-element.9, f32[512]{0:T(512)S(1)} %add_sqrt_fusion.3), kind=kLoop, calls=%fused_computation.75 | loop fusion | flops 1179648 | bytes 3540992 | tf_op jit(solution)/shard_map/convert_element_type | solution.py:83
  21.6 3.2 %multiply_reduce_fusion.3 = (f32[512]{0:T(512)S(1)}, f32[512,1152]{1,0:T(8,128)S(1)}) fusion(bf16[512,1152]{1,0:T(8,128)(2,1)} %collective-permute-done.1, bf16[1152,1152]{1,0:T(8,128)(2,1)S(1)} %copy-done), kind=kOutput, calls=%fused_computation.18 | convolution fusion | flops 1360133632 | bytes 6195200 | tf_op jit(solution)/shard_map/dot_general | solution.py:37
  28.2 8.1 %collective-permute-done = bf16[512,1152]{1,0:T(8,128)(2,1)} collective-permute-done((bf16[512,1152]{1,0:T(8,128)(2,1)}, bf16[512,1152]{1,0:T(8,128)(2,1)}, u32[]{:S(2)}, u32[]{:S(2)}) %collective-permute-start) | collective-permute-done | bytes 1179680 | tf_op jit(solution)/shard_map/ppermute | solution.py:33
  36.3 3.2 %multiply_reduce_fusion.5 = (f32[512]{0:T(512)S(1)}, f32[512,1152]{1,0:T(8,128)S(1)}) fusion(bf16[512,1152]{1,0:T(8,128)(2,1)} %collective-permute-done, bf16[1152,1152]{1,0:T(8,128)(2,1)S(1)} %copy-done.5), kind=kOutput, calls=%fused_computation.21 | convolution fusion | flops 1360133632 | bytes 6195200 | tf_op jit(solution)/shard_map/dot_general | solution.py:37
  43.5 1.2 fusion.21
  46.6 1.2 multiply_reduce_fusion.1
  50.2 3.3 %fusion.23 = f32[1152,1152]{1,0:T(8,128)S(1)} fusion(bf16[512,1152]{1,0:T(8,128)(2,1)} %get-tuple-element.6, f32[512,1152]{1,0:T(8,128)S(1)} %get-tuple-element.21, f32[512]{0:T(512)S(1)} %get-tuple-element.20, f32[512]{0:T(512)S(1)} %add_sqrt_fusion.3, f32[512,1152]{1,0:T(8,128)S(1)} %copy-done.3), kind=kOutput, calls=%fused_computation.47 | convolution fusion | flops 1361903616 | bytes 11210752 | tf_op jit(solution)/shard_map/dot_general | solution.py:45
  53.5 3.3 %fusion.24 = f32[1152,1152]{1,0:T(8,128)S(1)} fusion(bf16[512,1152]{1,0:T(8,128)(2,1)} %get-tuple-element.7, f32[512,1152]{1,0:T(8,128)S(1)} %get-tuple-element.15, f32[512]{0:T(512)S(1)} %get-tuple-element.14, f32[512]{0:T(512)S(1)} %add_sqrt_fusion.2, f32[512,1152]{1,0:T(8,128)S(1)} %copy-done.2), kind=kOutput, calls=%fused_computation.48 | convolution fusion | flops 1361903616 | bytes 11210752 | tf_op jit(solution)/shard_map/dot_general | solution.py:45
  56.7 3.3 %convolution_add_fusion.1 = f32[1152,1152]{1,0:T(8,128)S(1)} fusion(f32[1152,1152]{1,0:T(8,128)S(1)} %fusion.23, bf16[512,1152]{1,0:T(8,128)(2,1)} %collective-permute-done.1, f32[512,1152]{1,0:T(8,128)S(1)} %get-tuple-element.23, f32[512]{0:T(512)S(1)} %get-tuple-element.22, f32[512]{0:T(512)S(1)} %add_sqrt_fusion, f32[512,1152]{1,0:T(8,128)S(1)} %get-tuple-element.13), kind=kOutput, calls=%fused_computation.1 | convolution fusion | flops 1363230720 | bytes 16519168 | tf_op jit(solution)/shard_map/dot_general | solution.py:45
  60.1 3.3 %select_convert_fusion = (bf16[1152,1152]{1,0:T(8,128)(2,1)S(1)}, f32[1152,1152]{1,0:T(8,128)S(1)}) fusion(f32[1152,1152]{1,0:T(8,128)S(1)} %convolution_add_fusion.1, pred[]{:T(512)S(6)} %eq.8, f32[1152,1152]{1,0:T(8,128)S(1)} %fusion.24, bf16[512,1152]{1,0:T(8,128)(2,1)} %collective-permute-done, f32[512,1152]{1,0:T(8,128)S(1)} %get-tuple-element.19, ...), kind=kOutput, calls=%fused_computation.3 | convolution fusion | flops 1364557824 | bytes 24481792 | tf_op jit(solution)/shard_map/dot_general | solution.py:45
  63.3 7.8 %collective-permute-start.2 = (bf16[1152,1152]{1,0:T(8,128)(2,1)S(1)}, bf16[1152,1152]{1,0:T(8,128)(2,1)S(1)}, u32[]{:S(2)}, u32[]{:S(2)}) collective-permute-start(bf16[1152,1152]{1,0:T(8,128)(2,1)S(1)} %get-tuple-element.24), channel_id=1, source_target_pairs={{0,1},{1,0},{2,3},{3,2},{4,5},{5,4},{6,7},{7,6},{8,9},{9,8},{10,11... | collective-permute-start | bytes 7962632 | tf_op jit(solution)/shard_map/ppermute | solution.py:112
  71.2 4.6 %collective-permute-done.2 = bf16[1152,1152]{1,0:T(8,128)(2,1)S(1)} collective-permute-done((bf16[1152,1152]{1,0:T(8,128)(2,1)S(1)}, bf16[1152,1152]{1,0:T(8,128)(2,1)S(1)}, u32[]{:S(2)}, u32[]{:S(2)}) %collective-permute-start.2) | collective-permute-done | bytes 2654240 | tf_op jit(solution)/shard_map/ppermute | solution.py:112
  76.6 3.1 %reshape.47 = bf16[4,8,4,9,1152]{4,3,2,1,0:T(8,128)(2,1)} reshape(bf16[1152,1152]{1,0:T(8,128)(2,1)S(1)} %add_convert_fusion) | data formatting | bytes 5308416 | tf_op jit(solution)/shard_map/reshape | solution.py:113
  79.7 5.0 %copy.12 = bf16[4,4,8,9,1152]{4,3,2,1,0:T(8,128)(2,1)} copy(bf16[4,4,8,9,1152]{4,3,1,2,0:T(8,128)(2,1)} %bitcast.44) | data formatting | bytes 5308416 | tf_op jit(solution)/shard_map/reshape | solution.py:113
  84.7 5.7 %reshape.51 = bf16[16,72,1152]{2,1,0:T(8,128)(2,1)} reshape(bf16[4,4,8,9,1152]{4,3,2,1,0:T(8,128)(2,1)} %copy.12) | data formatting | bytes 5308416 | tf_op jit(solution)/shard_map/reshape | solution.py:113
  90.5 38.7 %all_to_all.10 = bf16[16,72,1152]{2,1,0:T(8,128)(2,1)} all-to-all(bf16[16,72,1152]{2,1,0:T(8,128)(2,1)} %reshape.51), channel_id=1, replica_groups={{0,2,4,6,64,66,68,70,128,130,132,134,192,194,196,198},{1,3,5,7,65,67,69..., dimensions={0} | all-to-all | bytes 5308416 | tf_op jit(solution)/shard_map/all_to_all | solution.py:114
  129.2 2.2 %reduce_sum.101 = bf16[72,1152]{1,0:T(8,128)(2,1)S(1)} reduce(bf16[16,72,1152]{2,1,0:T(8,128)(2,1)} %all_to_all.10, bf16[]{:T(256)} %constant.34.clone.1), dimensions={0}, to_apply=%region_8.9 | reduce | flops 1244160 | bytes 2820098 | tf_op jit(solution)/shard_map/reduce_sum | solution.py:115
  132.1 3.4 %all-to-all-start.1 = ((bf16[8,9,1152]{2,1,0:T(8,128)(2,1)}), bf16[8,9,1152]{2,1,0:T(8,128)(2,1)S(1)}, u32[]{:S(2)}, u32[]{:S(2)}) async-start(bf16[8,9,1152]{2,1,0:T(8,128)(2,1)} %reshape.49), calls=%async_computation.1 | async-start | bytes 589824 | tf_op jit(solution)/shard_map/all_to_all | solution.py:116
  135.6 10.5 %all-to-all-done.1 = bf16[8,9,1152]{2,1,0:T(8,128)(2,1)S(1)} async-done(((bf16[8,9,1152]{2,1,0:T(8,128)(2,1)}), bf16[8,9,1152]{2,1,0:T(8,128)(2,1)S(1)}, u32[]{:S(2)}, u32[]{:S(2)}) %all-to-all-start.1) | async-done | bytes 165920 | tf_op jit(solution)/shard_map/all_to_all | solution.py:116
  146.4 3.0 %collective-permute-start.3 = (f32[5184]{0:T(1024)S(1)}, f32[5184]{0:T(1024)S(1)}, u32[]{:S(2)}, u32[]{:S(2)}) collective-permute-start(f32[5184]{0:T(1024)S(1)} %get-tuple-element.2), channel_id=1, source_target_pairs={{0,1},{1,0},{2,3},{3,2},{4,5},{5,4},{6,7},{7,6},{8,9},{9,8},{10,11... | collective-permute-start | bytes 62216 | tf_op jit(solution)/shard_map/ppermute | solution.py:119
  (38 shorter events, 16.0 us)
Async XLA Ops:
  0.6 7.4 %copy-start = (bf16[1152,1152]{1,0:T(8,128)(2,1)S(1)}, bf16[1152,1152]{1,0:T(8,128)(2,1)}, u32[]{:S(2)}) copy-start(bf16[1152,1152]{1,0:T(8,128)(2,1)} %param.9) | copy-start | bytes 7962628
  4.8 16.8 %collective-permute-start.1 = (bf16[512,1152]{1,0:T(8,128)(2,1)}, bf16[512,1152]{1,0:T(8,128)(2,1)}, u32[]{:S(2)}, u32[]{:S(2)}) collective-permute-start(bf16[512,1152]{1,0:T(8,128)(2,1)} %get-tuple-element.6), channel_id=1, source_target_pairs={{0,255},{1,0},{2,1},{3,2},{4,3},{5,4},{6,5},{7,6},{8,7},{9,8},{10,... | collective-permute-start | bytes 3538952 | tf_op jit(solution)/shard_map/ppermute | solution.py:33
  8.1 4.7 %copy-start.4 = (bf16[1152,1152]{1,0:T(8,128)(2,1)S(1)}, bf16[1152,1152]{1,0:T(8,128)(2,1)}, u32[]{:S(2)}) copy-start(bf16[1152,1152]{1,0:T(8,128)(2,1)} %param.10) | copy-start | bytes 7962628
  8.1 28.2 %collective-permute-start = (bf16[512,1152]{1,0:T(8,128)(2,1)}, bf16[512,1152]{1,0:T(8,128)(2,1)}, u32[]{:S(2)}, u32[]{:S(2)}) collective-permute-start(bf16[512,1152]{1,0:T(8,128)(2,1)} %get-tuple-element.7), channel_id=1, source_target_pairs={{0,2},{1,3},{2,4},{3,5},{4,6},{5,7},{6,8},{7,9},{8,10},{9,11},{10,... | collective-permute-start | bytes 3538952 | tf_op jit(solution)/shard_map/ppermute | solution.py:33
  20.6 4.3 %copy-start.2 = (f32[512,1152]{1,0:T(8,128)S(1)}, f32[512,1152]{1,0:T(8,128)}, u32[]{:S(2)}) copy-start(f32[512,1152]{1,0:T(8,128)} %get-tuple-element.11) | copy-start | bytes 7077892
  27.3 9.0 %copy-start.5 = (bf16[1152,1152]{1,0:T(8,128)(2,1)S(1)}, bf16[1152,1152]{1,0:T(8,128)(2,1)}, u32[]{:S(2)}) copy-start(bf16[1152,1152]{1,0:T(8,128)(2,1)} %param.10) | copy-start | bytes 7962628
  40.8 1.7 %copy-start.3 = (f32[512,1152]{1,0:T(8,128)S(1)}, f32[512,1152]{1,0:T(8,128)}, u32[]{:S(2)}) copy-start(f32[512,1152]{1,0:T(8,128)} %get-tuple-element.9) | copy-start | bytes 7077892
  63.3 12.4 %collective-permute-start.2 = (bf16[1152,1152]{1,0:T(8,128)(2,1)S(1)}, bf16[1152,1152]{1,0:T(8,128)(2,1)S(1)}, u32[]{:S(2)}, u32[]{:S(2)}) collective-permute-start(bf16[1152,1152]{1,0:T(8,128)(2,1)S(1)} %get-tuple-element.24), channel_id=1, source_target_pairs={{0,1},{1,0},{2,3},{3,2},{4,5},{5,4},{6,7},{7,6},{8,9},{9,8},{10,11... | collective-permute-start | bytes 7962632 | tf_op jit(solution)/shard_map/ppermute | solution.py:112
  90.5 60.4 %copy-start.1 = (bf16[1152,1152]{1,0:T(8,128)(2,1)S(1)}, bf16[1152,1152]{1,0:T(8,128)(2,1)}, u32[]{:S(2)}) copy-start(bf16[1152,1152]{1,0:T(8,128)(2,1)} %param.9) | copy-start | bytes 7962628
  132.1 14.0 %all-to-all-start.1 = ((bf16[8,9,1152]{2,1,0:T(8,128)(2,1)}), bf16[8,9,1152]{2,1,0:T(8,128)(2,1)S(1)}, u32[]{:S(2)}, u32[]{:S(2)}) async-start(bf16[8,9,1152]{2,1,0:T(8,128)(2,1)} %reshape.49), calls=%async_computation.1 | async-start | bytes 589824 | tf_op jit(solution)/shard_map/all_to_all | solution.py:116
  146.4 3.8 %collective-permute-start.3 = (f32[5184]{0:T(1024)S(1)}, f32[5184]{0:T(1024)S(1)}, u32[]{:S(2)}, u32[]{:S(2)}) collective-permute-start(f32[5184]{0:T(1024)S(1)} %get-tuple-element.2), channel_id=1, source_target_pairs={{0,1},{1,0},{2,3},{3,2},{4,5},{5,4},{6,7},{7,6},{8,9},{9,8},{10,11... | collective-permute-start | bytes 62216 | tf_op jit(solution)/shard_map/ppermute | solution.py:119

commit v2 on v1

v2 whole, which is shorter than its diff:
```python
import functools

import jax
import jax.numpy as jnp
import numpy as np
from jax import lax
from jax.experimental import pallas as pl
from jax.experimental.pallas import tpu as pltpu
from jax.sharding import PartitionSpec as P

BLK = 128
D = 1152
R = 512
NY, NZ, NX = 4, 8, 4
N = 256
OWN = 9
COLS = 384
ROWS = 256
BF = jnp.bfloat16
F32 = jnp.float32
VMEM = pl.BlockSpec(memory_space=pltpu.VMEM)
SMEM = pl.BlockSpec(memory_space=pltpu.SMEM)


def dev(y, z, x, c):
    return ((y * NZ + z) * NX + x) * 2 + c


PLANES = [
    [dev(y, z, x, c) for y in range(NY) for x in range(NX)]
    for z in range(NZ)
    for c in range(2)
]
COLUMNS = [
    [dev(y, z, x, c) for z in range(NZ)]
    for y in range(NY)
    for x in range(NX)
    for c in range(2)
]
SWAP = [(d, d ^ 1) for d in range(N)]


def shuffle_matrix():
    flat = np.arange(D).reshape(NY, NZ, NX, OWN)
    source = flat.transpose(0, 2, 1, 3).reshape(-1)
    matrix = np.zeros((D, D), np.float32)
    matrix[np.arange(D), source] = 1.0
    return jnp.asarray(matrix, BF)


def shift(value, steps):
    return lax.ppermute(value, "dp", [(d, (d + steps) % N) for d in range(N)])


def mm(a, b):
    return jnp.dot(a, b, preferred_element_type=F32)


def mm_t(a, b):
    return lax.dot_general(a, b, (((1,), (1,)), ((), ())), preferred_element_type=F32)


def t_mm(a, b):
    return lax.dot_general(a, b, (((0,), (0,)), ((), ())), preferred_element_type=F32)


def cols(j):
    return pl.ds(pl.multiple_of(j * COLS, 128), COLS)


def project(feat_ref, proj_ref, dir_ref, unit_ref, inv_ref):
    def product(j, squares):
        raw = mm(feat_ref[...], proj_ref[:, cols(j)])
        dir_ref[:, cols(j)] = raw
        return squares + jnp.sum(raw * raw, axis=1, keepdims=True)

    squares = lax.fori_loop(0, D // COLS, product, jnp.zeros((R, 1), F32))
    inv_ref[...] = 1.0 / jnp.sqrt(squares + 1e-06)

    @pl.loop(0, R // ROWS)
    def _(i):
        rows = pl.ds(pl.multiple_of(i * ROWS, ROWS), ROWS)
        direction = dir_ref[rows, :] * inv_ref[rows, :]
        dir_ref[rows, :] = direction
        unit_ref[rows, :] = direction.astype(BF)


def turned(feat_ref, shuffle_ref, out_ref):
    @pl.loop(0, D // COLS)
    def _(j):
        rows = pl.ds(pl.multiple_of(j * COLS, COLS), COLS)
        out_ref[rows, :] = mm_t(shuffle_ref[rows, :], feat_ref[...]).astype(BF)


def raw_grad(gradient, direction, inverse):
    radial = jnp.sum(direction * gradient, axis=1, keepdims=True)
    return ((gradient - direction * radial) * inverse).astype(BF)


def weights(image_unit, text_unit, scale, bias):
    return scale * mm_t(image_unit, text_unit) + bias


def first_kernel(text, image, text_proj, image_proj, shuffle,
                 dir_t, unit_t, inv_t, turn_t, dir_i, unit_i, inv_i, turn_i):
    project(text, text_proj, dir_t, unit_t, inv_t)
    project(image, image_proj, dir_i, unit_i, inv_i)
    turned(text, shuffle, turn_t)
    turned(image, shuffle, turn_i)


def text_side(pair_ref, unit_i0, unit_i1, dir_t, inv_t, out_ref, scratch, scale):
    @pl.loop(0, D // COLS)
    def _(j):
        scratch[:, cols(j)] = scale * (
            t_mm(pair_ref[:R, :], unit_i0[:, cols(j)])
            + t_mm(pair_ref[R:, :], unit_i1[:, cols(j)])
        )

    @pl.loop(0, R // ROWS)
    def _(i):
        rows = pl.ds(pl.multiple_of(i * ROWS, ROWS), ROWS)
        out_ref[rows, :] = raw_grad(scratch[rows, :], dir_t[rows, :], inv_t[rows, :])


def second_kernel(scal, image1, image_proj, shuffle, unit_i0, unit_t0, dir_t0, inv_t0,
                  dir_i1, unit_i1, inv_i1, turn_i1, grad_i, delta_t0, pair, scratch):
    scale, bias = scal[0], scal[1]
    project(image1, image_proj, dir_i1, unit_i1, inv_i1)

    @pl.loop(0, R // ROWS)
    def _(i):
        rows = pl.ds(pl.multiple_of(i * ROWS, ROWS), ROWS)
        logit = weights(unit_i0[rows, :], unit_t0[...], scale, bias)
        at = lax.broadcasted_iota(jnp.int32, logit.shape, 0) + i * ROWS
        sign = jnp.where(at == lax.broadcasted_iota(jnp.int32, logit.shape, 1), -1.0, 1.0)
        weight = (sign * jax.nn.sigmoid(sign * logit)).astype(BF)
        pair[rows, :] = weight
        grad_i[rows, :] = mm(weight, unit_t0[...])

    @pl.loop(0, R // ROWS)
    def _(i):
        rows = pl.ds(pl.multiple_of(i * ROWS, ROWS), ROWS)
        below = pl.ds(pl.multiple_of(R + i * ROWS, ROWS), ROWS)
        weight = jax.nn.sigmoid(weights(unit_i1[rows, :], unit_t0[...], scale, bias)).astype(BF)
        pair[below, :] = weight
        grad_i[below, :] = mm(weight, unit_t0[...])

    text_side(pair, unit_i0, unit_i1, dir_t0, inv_t0, delta_t0, scratch, scale)
    turned(image1, shuffle, turn_i1)


def third_kernel(scal, text2, text_proj, shuffle, unit_i0, unit_i1, dir_i0, dir_i1, inv_i0, inv_i1,
                 grad_i, delta_i, delta_t2, turn_t2, dir_t2, unit_t2, inv_t2, pair, scratch):
    scale, bias = scal[0], scal[1]
    project(text2, text_proj, dir_t2, unit_t2, inv_t2)
    for unit_i, dir_i, inv_i, base in (
        (unit_i0, dir_i0, inv_i0, 0),
        (unit_i1, dir_i1, inv_i1, R),
    ):
        @pl.loop(0, R // ROWS)
        def _(i):
            rows = pl.ds(pl.multiple_of(i * ROWS, ROWS), ROWS)
            below = pl.ds(pl.multiple_of(base + i * ROWS, ROWS), ROWS)
            weight = jax.nn.sigmoid(weights(unit_i[rows, :], unit_t2[...], scale, bias)).astype(BF)
            pair[below, :] = weight
            gradient = scale * (grad_i[below, :] + mm(weight, unit_t2[...]))
            delta_i[below, :] = raw_grad(gradient, dir_i[rows, :], inv_i[rows, :])

    text_side(pair, unit_i0, unit_i1, dir_t2, inv_t2, delta_t2, scratch, scale)
    turned(text2, shuffle, turn_t2)


def term_kernel(image_row, which, turn_i0, turn_i1, delta_i, turn_t0, turn_t2, delta_t0, delta_t2, out):
    def total(turn_a, turn_b, delta_a, delta_b):
        @pl.loop(0, D // COLS)
        def _(j):
            out[:, cols(j)] = (
                mm(turn_a[...], delta_a[:, cols(j)]) + mm(turn_b[...], delta_b[:, cols(j)])
            ).astype(out.dtype)

    @pl.when(which[0] == image_row)
    def _():
        total(turn_i0, turn_i1, delta_i.at[:R], delta_i.at[R:])

    @pl.when(which[0] != image_row)
    def _():
        total(turn_t0, turn_t2, delta_t0, delta_t2)


def call(kernel, operands, outs, scratch=(), flops=0, name=None):
    shapes = [jax.ShapeDtypeStruct(shape, kind) for shape, kind in outs]
    moved = sum(a.size * a.dtype.itemsize for a in operands)
    moved += sum(int(np.prod(s.shape)) * s.dtype.itemsize for s in shapes)
    return pl.pallas_call(
        kernel,
        out_shape=shapes,
        in_specs=[SMEM if a.size < 8 else VMEM for a in operands],
        out_specs=[VMEM] * len(shapes),
        scratch_shapes=[pltpu.VMEM(shape, kind) for shape, kind in scratch],
        compiler_params=pltpu.CompilerParams(vmem_limit_bytes=40 << 20),
        cost_estimate=pl.CostEstimate(flops=flops, bytes_accessed=moved, transcendentals=0),
        name=name,
    )(*operands)


def local(image_feat, text_feat, image_proj, text_proj, logit_scale_logarithm, bias, counts):
    scal = jnp.stack([jnp.exp(logit_scale_logarithm[0]), bias[0]])
    rows = lax.broadcasted_iota(jnp.int32, image_feat.shape, 0)
    live = rows < counts[0] * BLK
    zero = jnp.zeros((), BF)
    text0 = jnp.where(live, text_feat, zero)
    image_feat, text0 = lax.optimization_barrier((image_feat, text0))
    image0 = jnp.where(live, image_feat, zero)
    text2 = shift(text0, 2)
    image1 = shift(image0, -1)
    shuffle = shuffle_matrix()

    unit, wide, line, turn = ((R, D), BF), ((R, D), F32), ((R, 1), F32), ((D, R), BF)
    step = 2 * R * D * D
    dir_t0, unit_t0, inv_t0, turn_t0, dir_i0, unit_i0, inv_i0, turn_i0 = call(
        first_kernel,
        (text0, image0, text_proj, image_proj, shuffle),
        [wide, unit, line, turn] * 2,
        flops=4 * step,
        name="own_rows",
    )
    dir_i1, unit_i1, inv_i1, turn_i1, grad_i, delta_t0 = call(
        second_kernel,
        (scal, image1, image_proj, shuffle, unit_i0, unit_t0, dir_t0, inv_t0),
        [wide, unit, line, turn, ((2 * R, D), F32), unit],
        [((2 * R, R), BF), ((R, D), F32)],
        flops=5 * step,
        name="own_texts",
    )
    delta_i, delta_t2, turn_t2 = call(
        third_kernel,
        (scal, text2, text_proj, shuffle, unit_i0, unit_i1, dir_i0, dir_i1, inv_i0, inv_i1, grad_i),
        [((2 * R, D), BF), unit, turn],
        [wide, unit, line, ((2 * R, R), BF), wide],
        flops=5 * step,
        name="far_texts",
    )

    core = lax.axis_index("dp") % 2
    which = core.reshape(1)
    terms = (which, turn_i0, turn_i1, delta_i, turn_t0, turn_t2, delta_t0, delta_t2)
    (away,) = call(functools.partial(term_kernel, 1), terms, [((D, D), BF)], flops=2 * step, name="away")
    back = lax.ppermute(away, "dp", SWAP)
    (kept,) = call(functools.partial(term_kernel, 0), terms, [((D, D), F32)], flops=2 * step, name="kept")
    chip = (kept + back.astype(F32)).astype(BF).reshape(NY * NX, NZ * OWN, D)
    plane = lax.all_to_all(chip, "dp", 0, 0, axis_index_groups=PLANES, tiled=True)
    plane = jnp.sum(plane.astype(F32), axis=0).astype(BF).reshape(NZ, OWN, D)
    column = lax.all_to_all(plane, "dp", 0, 0, axis_index_groups=COLUMNS, tiled=True)
    total = jnp.sum(column.astype(F32), axis=0).reshape(2, OWN * D // 2)
    first = core == 0
    mine = lax.dynamic_index_in_dim(total, core, 0, False)
    other = lax.ppermute(lax.dynamic_index_in_dim(total, 1 - core, 0, False), "dp", SWAP)
    return jnp.where(first, mine, other), jnp.where(first, other, mine)


def solution(mesh):
    return jax.shard_map(
        local,
        mesh=mesh,
        in_specs=(P("dp", None), P("dp", None), P(), P(), P(), P(), P("dp")),
        out_specs=(P("dp"), P("dp")),
        check_vma=False,
    )
```

time: 152 us -> 146 us (0.961)
  Pallas kernels: 0 us -> 58.4 us
  matrix products: 41.1 us -> 0 us
  waiting for transfers between devices: 25.1 us -> 11.5 us
  local copies, waits for them, and re-layouts: 15.7 us -> 8.54 us
  starting transfers between devices: 17.5 us -> 21.7 us
  other arithmetic: 9.72 us -> 5.93 us
    pallas_call x0 -> x5, Pallas kernels: none -> 58.4 us  [call(): pl.pallas_call(kernel, out_shape=shapes, in_specs=[SMEM if a.size < 8 els...]
    dot_general x20 -> x0, matrix products: 41.1 us -> none  [the longest x8 19.5 us: mm(): return jnp.dot(a, b, preferred_element_type=F32)]
    reshape x5 -> x2, local copies, waits for them, and re-layouts: 14.8 us -> 0.88 us  [the longest x1 0.78 us: local(): plane = jnp.sum(plane.astype(F32), axis=0).astype(BF).reshape(NZ, OWN, D)]
    ppermute x2, waiting for transfers between devices: 9.16 us -> 0.01 us  [shift(): return lax.ppermute(value, 'dp', [(d, (d + steps) % N) for d in range(N)])]
    unnamed x12 -> x14, local copies, waits for them, and re-layouts: 0.81 us -> 7.54 us
    ppermute x1, waiting for transfers between devices: 4.58 us -> 0.01 us  [local(): back = lax.ppermute(away, 'dp', SWAP)]
    all_to_all x1, starting transfers between devices: 3.42 us -> 6.89 us  [local(): lax.all_to_all(plane, 'dp', 0, 0, axis_index_groups=COLUMNS, tiled=True)]
    select_n x1, other arithmetic: 3.37 us -> 0.2 us  [local(): image0 = jnp.where(live, image_feat, zero)]
  transfers between devices with their start and end apart: 5 -> 5, of which waited for: 5 -> 2; matrix products, arithmetic and copies ran while one was open for 12% -> 0% of each run, Pallas kernels for 0% -> 26%
where the time goes in v2:
time: 146 us
  Pallas kernels  58.4 us (40%)
  blocking collectives  37.3 us (26%)
  starting transfers between devices  21.7 us (15%)
  waiting for transfers between devices  11.5 us (8%)
  local copies, waits for them, and re-layouts  8.54 us (6%)
  other arithmetic  5.93 us (4%)
  between operations  2.71 us (2%)
    pallas_call x5, Pallas kernels, call(): pl.pallas_call(kernel, out_shape=shapes, in_specs=[SMEM if a.size < 8 els...  58.4 us
    all_to_all x1, blocking collectives, local(): lax.all_to_all(chip, 'dp', 0, 0, axis_index_groups=PLANES, tiled=True)  37.3 us
    all_to_all x1, waiting for transfers between devices, local(): lax.all_to_all(plane, 'dp', 0, 0, axis_index_groups=COLUMNS, tiled=True)  10.6 us
    ppermute x1, starting transfers between devices, local(): back = lax.ppermute(away, 'dp', SWAP)  8.48 us
    unnamed x14, local copies, waits for them, and re-layouts  7.54 us
    all_to_all x1, starting transfers between devices, local(): lax.all_to_all(plane, 'dp', 0, 0, axis_index_groups=COLUMNS, tiled=True)  6.89 us
    ppermute x2, starting transfers between devices, shift(): return lax.ppermute(value, 'dp', [(d, (d + steps) % N) for d in range(N)])  3.32 us
    convert_element_type x1, other arithmetic, local(): chip = (kept + back.astype(F32)).astype(BF).reshape(NY * NX, NZ * OWN, D)  3 us
  transfers between devices with their start and end apart: 5, of which 2 were waited for; matrix products, arithmetic and copies ran while one was open for 0% of the time, Pallas kernels for 26%

profile of v2, /device:TPU:1, one launch (start us, length us, event | category | flops | bytes accessed | tf_op | source)
XLA Modules:
  0.0 146.0 jit_solution(15029445984230113922)
XLA Ops:
  1.3 1.6 %broadcast_select_fusion.1.text = bf16[512,1152]{1,0:T(8,128)(2,1)S(1)} fusion(bf16[512,1152]{1,0:T(8,128)(2,1)} %param.9, pred[512]{0:T(512)(128)(4,1)S(1)} %iota_compare_fusion), kind=kLoop, calls=%fused_computation.2 | loop fusion | flops 589824 | bytes 2359808 | tf_op jit(solution)/shard_map/jit(_where)/select_n | solution.py:212
  2.9 0.2 broadcast_select_fusion.image
  3.1 3.3 %collective-permute-start = (bf16[512,1152]{1,0:T(8,128)(2,1)S(1)}, bf16[512,1152]{1,0:T(8,128)(2,1)}, u32[]{:S(2)}, u32[]{:S(2)}) collective-permute-start(bf16[512,1152]{1,0:T(8,128)(2,1)S(1)} %broadcast_select_fusion.image), channel_id=1, source_target_pairs={{0,255},{1,0},{2,1},{3,2},{4,3},{5,4},{6,5},{7,6},{8,7},{9,8},{10,... | collective-permute-start | bytes 3538952 | tf_op jit(solution)/shard_map/ppermute | solution.py:52
  7.9 13.9 %own_rows.1 = (f32[512,1152]{1,0:T(8,128)S(1)}, bf16[512,1152]{1,0:T(8,128)(2,1)S(1)}, f32[512,1]{1,0:T(8,128)S(1)}, bf16[1152,512]{1,0:T(8,128)(2,1)S(1)}, f32[...) custom-call(bf16[512,1152]{1,0:T(8,128)(2,1)S(1)} %broadcast_select_f, ...), custom_call_target="tpu_custom_call" | custom-call | flops 5435817984 | bytes 19763200 | tf_op jit(solution)/shard_map/own_rows/pallas_call | solution.py:195
  21.8 1.4 copy-done
  23.2 17.0 %own_texts.1 = (f32[512,1152]{1,0:T(8,128)S(1)}, bf16[512,1152]{1,0:T(8,128)(2,1)S(1)}, f32[512,1]{1,0:T(8,128)S(1)}, bf16[1152,512]{1,0:T(8,128)(2,1)S(1)}, f32...) custom-call(f32[2]{0:T(128)S(1)} %pad_maximum_fusion.scal, bf16[512,1152]{1,0:T(8,128)(2,1)} %collective-permute-done.image1, ...), custom_call_target="tpu_custom_call" | custom-call | flops 6794772480 | bytes 21827592 | tf_op jit(solution)/shard_map/own_texts/pallas_call | solution.py:195
  40.2 1.5 %copy-done.2 = f32[512,1152]{1,0:T(8,128)} copy-done((f32[512,1152]{1,0:T(8,128)}, f32[512,1152]{1,0:T(8,128)S(1)}, u32[]{:S(2)}) %copy-start.2) | copy-done | bytes 2359320
  41.7 1.7 %copy-done.1 = f32[512,1152]{1,0:T(8,128)S(1)} copy-done((f32[512,1152]{1,0:T(8,128)S(1)}, f32[512,1152]{1,0:T(8,128)}, u32[]{:S(2)}) %copy-start.1) | copy-done | bytes 2359320
  43.3 1.7 %copy-done.3 = f32[512,1152]{1,0:T(8,128)S(1)} copy-done((f32[512,1152]{1,0:T(8,128)S(1)}, f32[512,1152]{1,0:T(8,128)}, u32[]{:S(2)}) %copy-start.3) | copy-done | bytes 2359320
  45.0 1.3 copy-done.5
  46.3 16.8 %far_texts.1 = (bf16[1024,1152]{1,0:T(8,128)(2,1)S(1)}, bf16[512,1152]{1,0:T(8,128)(2,1)S(1)}, bf16[1152,512]{1,0:T(8,128)(2,1)S(1)}) custom-call(f32[2]{0:T(128)S(1)} %pad_maximum_fusion.scal, bf16[512,1152]{1,0:T(8,128)(2,1)S(1)} %collective-permute-done.1.text2, bf16[1152,1152]{1,0:T(8,128)(2,1)} %text_proj.3, bf16[1152,1152]{1,0:T(8,128)(2,1)} %constant.37.clone.shuffle, ...), custom_call_target="tpu_custom_call" | custom-call | flops 6794772480 | bytes 23007240 | tf_op jit(solution)/shard_map/far_texts/pallas_call | solution.py:195
  63.1 4.2 %away.1 = bf16[1152,1152]{1,0:T(8,128)(2,1)S(1)} custom-call(s32[1]{0:T(128)} %bitcast.which, bf16[1152,512]{1,0:T(8,128)(2,1)S(1)} %get-tuple-element.23.turn_i0, bf16[1152,512]{1,0:T(8,128)(2,1)S(1)} %get-tuple-element.28.turn_i1, bf16[1024,1152]{1,0:T(8,128)(2,1)S(1)} %get-tuple-element.35.delta_i, bf16[1152,512]{1,0:T(8,128)(2,1)S(1)} %get-tuple-element.36.turn_t0, ...), custom_call_target="tpu_custom_call" | custom-call | flops 2717908992 | bytes 12091396 | tf_op jit(solution)/shard_map/away/pallas_call | solution.py:195
  67.3 8.5 %collective-permute-start.2 = (bf16[1152,1152]{1,0:T(8,128)(2,1)S(1)}, bf16[1152,1152]{1,0:T(8,128)(2,1)S(1)}, u32[]{:S(2)}, u32[]{:S(2)}) collective-permute-start(bf16[1152,1152]{1,0:T(8,128)(2,1)S(1)} %away.1), channel_id=1, source_target_pairs={{0,1},{1,0},{2,3},{3,2},{4,5},{5,4},{6,7},{7,6},{8,9},{9,8},{10,11... | collective-permute-start | bytes 7962632 | tf_op jit(solution)/shard_map/ppermute | solution.py:249
  75.8 6.5 %kept.1 = f32[1152,1152]{1,0:T(8,128)} custom-call(s32[1]{0:T(128)} %bitcast.which, bf16[1152,512]{1,0:T(8,128)(2,1)S(1)} %get-tuple-element.23.turn_i0, bf16[1152,512]{1,0:T(8,128)(2,1)S(1)} %get-tuple-element.28.turn_i1, bf16[1024,1152]{1,0:T(8,128)(2,1)S(1)} %get-tuple-element.35.delta_i, bf16[1152,512]{1,0:T(8,128)(2,1)S(1)} %get-tuple-element.36.turn_t0, ...), custom_call_target="tpu_custom_call" | custom-call | flops 2717908992 | bytes 14745604 | tf_op jit(solution)/shard_map/kept/pallas_call | solution.py:195
  82.3 3.0 %add_convert_fusion = bf16[1152,1152]{1,0:T(8,128)(2,1)S(1)} fusion(f32[1152,1152]{1,0:T(8,128)} %kept.1, bf16[1152,1152]{1,0:T(8,128)(2,1)S(1)} %collective-permute-done.2), kind=kLoop, calls=%fused_computation | loop fusion | flops 3981312 | bytes 10616832 | tf_op jit(solution)/shard_map/convert_element_type | solution.py:251
  85.3 37.3 %all_to_all.10 = bf16[16,72,1152]{2,1,0:T(8,128)(2,1)S(1)} all-to-all(bf16[16,72,1152]{2,1,0:T(8,128)(2,1)S(1)} %bitcast.3), channel_id=1, replica_groups={{0,2,4,6,64,66,68,70,128,130,132,134,192,194,196,198},{1,3,5,7,65,67,69..., dimensions={0} | all-to-all | bytes 5308416 | tf_op jit(solution)/shard_map/all_to_all | solution.py:252
  122.6 0.4 reduce_sum.21
  123.0 0.8 reshape.22
  123.8 6.9 %all-to-all-start.1 = ((bf16[8,9,1152]{2,1,0:T(8,128)(2,1)}), bf16[8,9,1152]{2,1,0:T(8,128)(2,1)S(1)}, u32[]{:S(2)}, u32[]{:S(2)}) async-start(bf16[8,9,1152]{2,1,0:T(8,128)(2,1)} %reshape.22), calls=%async_computation.1 | async-start | bytes 589824 | tf_op jit(solution)/shard_map/all_to_all | solution.py:254
  130.6 10.6 %all-to-all-done.1 = bf16[8,9,1152]{2,1,0:T(8,128)(2,1)S(1)} async-done(((bf16[8,9,1152]{2,1,0:T(8,128)(2,1)}), bf16[8,9,1152]{2,1,0:T(8,128)(2,1)S(1)}, u32[]{:S(2)}, u32[]{:S(2)}) %all-to-all-start.1) | async-done | bytes 165920 | tf_op jit(solution)/shard_map/all_to_all | solution.py:254
  141.4 0.1 dynamic-slice_reduce_fusion
  141.6 3.0 %collective-permute-start.3 = (f32[5184]{0:T(1024)S(1)}, f32[5184]{0:T(1024)S(1)}, u32[]{:S(2)}, u32[]{:S(2)}) collective-permute-start(f32[5184]{0:T(1024)S(1)} %get-tuple-element.40), channel_id=1, source_target_pairs={{0,1},{1,0},{2,3},{3,2},{4,5},{5,4},{6,7},{7,6},{8,9},{9,8},{10,11... | collective-permute-start | bytes 62216 | tf_op jit(solution)/shard_map/ppermute | solution.py:258
  144.6 0.8 collective-permute-done.3
  145.4 0.6 broadcast_select_fusion.2
  (17 shorter events, 0.3 us)
Async XLA Ops:
  1.3 1.6 %copy-start.6 = (bf16[512,1152]{1,0:T(8,128)(2,1)S(1)}, bf16[512,1152]{1,0:T(8,128)(2,1)}, u32[]{:S(2)}) copy-start(bf16[512,1152]{1,0:T(8,128)(2,1)} %param.8) | copy-start | bytes 3538948
  3.1 20.1 %collective-permute-start = (bf16[512,1152]{1,0:T(8,128)(2,1)S(1)}, bf16[512,1152]{1,0:T(8,128)(2,1)}, u32[]{:S(2)}, u32[]{:S(2)}) collective-permute-start(bf16[512,1152]{1,0:T(8,128)(2,1)S(1)} %broadcast_select_fusion.image), channel_id=1, source_target_pairs={{0,255},{1,0},{2,1},{3,2},{4,3},{5,4},{6,5},{7,6},{8,7},{9,8},{10,... | collective-permute-start | bytes 3538952 | tf_op jit(solution)/shard_map/ppermute | solution.py:52
  6.4 35.2 %collective-permute-start.1 = (bf16[512,1152]{1,0:T(8,128)(2,1)S(1)}, bf16[512,1152]{1,0:T(8,128)(2,1)S(1)}, u32[]{:S(2)}, u32[]{:S(2)}) collective-permute-start(bf16[512,1152]{1,0:T(8,128)(2,1)S(1)} %broadcast_select_fusion.1.text), channel_id=1, source_target_pairs={{0,2},{1,3},{2,4},{3,5},{4,6},{5,7},{6,8},{7,9},{8,10},{9,11},{10,... | collective-permute-start | bytes 3538952 | tf_op jit(solution)/shard_map/ppermute | solution.py:52
  21.8 1.4 copy-start
  23.2 17.0 %copy-start.4 = (bf16[512,1152]{1,0:T(8,128)(2,1)}, bf16[512,1152]{1,0:T(8,128)(2,1)S(1)}, u32[]{:S(2)}) copy-start(bf16[512,1152]{1,0:T(8,128)(2,1)S(1)} %get-tuple-element.24.unit_i0) | copy-start | bytes 3538948
  40.2 1.5 %copy-start.2 = (f32[512,1152]{1,0:T(8,128)}, f32[512,1152]{1,0:T(8,128)S(1)}, u32[]{:S(2)}) copy-start(f32[512,1152]{1,0:T(8,128)S(1)} %get-tuple-element.31.dir_i1) | copy-start | bytes 7077892
  41.7 1.7 %copy-start.1 = (f32[512,1152]{1,0:T(8,128)S(1)}, f32[512,1152]{1,0:T(8,128)}, u32[]{:S(2)}) copy-start(f32[512,1152]{1,0:T(8,128)} %copy-done) | copy-start | bytes 7077892
  43.3 1.7 %copy-start.3 = (f32[512,1152]{1,0:T(8,128)S(1)}, f32[512,1152]{1,0:T(8,128)}, u32[]{:S(2)}) copy-start(f32[512,1152]{1,0:T(8,128)} %copy-done.2) | copy-start | bytes 7077892
  45.0 1.3 copy-start.5
  67.3 15.0 %collective-permute-start.2 = (bf16[1152,1152]{1,0:T(8,128)(2,1)S(1)}, bf16[1152,1152]{1,0:T(8,128)(2,1)S(1)}, u32[]{:S(2)}, u32[]{:S(2)}) collective-permute-start(bf16[1152,1152]{1,0:T(8,128)(2,1)S(1)} %away.1), channel_id=1, source_target_pairs={{0,1},{1,0},{2,3},{3,2},{4,5},{5,4},{6,7},{7,6},{8,9},{9,8},{10,11... | collective-permute-start | bytes 7962632 | tf_op jit(solution)/shard_map/ppermute | solution.py:249
  123.8 17.5 %all-to-all-start.1 = ((bf16[8,9,1152]{2,1,0:T(8,128)(2,1)}), bf16[8,9,1152]{2,1,0:T(8,128)(2,1)S(1)}, u32[]{:S(2)}, u32[]{:S(2)}) async-start(bf16[8,9,1152]{2,1,0:T(8,128)(2,1)} %reshape.22), calls=%async_computation.1 | async-start | bytes 589824 | tf_op jit(solution)/shard_map/all_to_all | solution.py:254
  141.6 3.8 %collective-permute-start.3 = (f32[5184]{0:T(1024)S(1)}, f32[5184]{0:T(1024)S(1)}, u32[]{:S(2)}, u32[]{:S(2)}) collective-permute-start(f32[5184]{0:T(1024)S(1)} %get-tuple-element.40), channel_id=1, source_target_pairs={{0,1},{1,0},{2,3},{3,2},{4,5},{5,4},{6,7},{7,6},{8,9},{9,8},{10,11... | collective-permute-start | bytes 62216 | tf_op jit(solution)/shard_map/ppermute | solution.py:258
